TPU v7x, 128 devices: a whole 4x4x4 slice. The times are simulated.
128 devices in a mesh: orb: 16 (over y_lo, z, core), dom: 8 (over y_hi, x).
Axes of the slice: x: 4, y: 4 (y_hi: 2, y_lo: 2; y = y_hi * 2 + y_lo), z: 4, core: 2. Of those that a mesh axis runs over, the one named last changes fastest.
Arguments:
- orbitals: float32 [128, 64, 64, 128], P('orb', 'dom'), may hold values from -6 to 6
- veff: float32 [64, 64, 128], P('dom'), may hold values from -1 to 0
- trials: float32 [16, 64, 64, 128], P('orb', 'dom'), may hold values from -32 to 32
- owners: int32 [2], replicated, may hold values from 0 to 15
- levels: float32 [8], replicated, may hold values from 0.05 to 1
- shift_index: int32 [128], P('orb'), may hold values from 0 to 7
Outputs:
- responses: float32 [16, 64, 64, 128], P('orb', 'dom')
Inputs may be any that keep to these rules, and one draw needn't show every extreme that they name: `owners`: an orbital group index. `shift_index`: an index into levels.
All inputs are finite; a program needn't handle non-finite values.
Results may differ from a plain program's by a relative error of at most 0.0001.
Values sent between devices are 32-bit elements; how exact they have to be, the bound alone decides.
A program may use at most 128 MiB of HBM per device.

v0:
```python
import jax
import jax.numpy as jnp
from jax import lax
from jax.sharding import PartitionSpec as P

APPS = 2
SWEEPS = 4


stencil_taps = (-49.0 / 18.0, 1.5, -0.15, 1.0 / 90.0)
center_shift = 4.05
center_depth = 5.05
inverse_half = 1.0 / 5.05
norm_epsilon = 1e-06


def extended_2(block, sides, width):
    for axis, dim in sides:
        count = lax.axis_size(axis)
        forward = [(i, i + 1) for i in range(count - 1)]
        backward = [(target, source) for source, target in forward]
        low = lax.ppermute(
            lax.slice_in_dim(block, block.shape[dim] - width, None, axis=dim), axis, forward
        )
        high = lax.ppermute(lax.slice_in_dim(block, 0, width, axis=dim), axis, backward)
        block = jnp.concatenate([low, block, high], axis=dim)
    return block


def spread(shard, axis, root):
    mine = lax.axis_index(axis) == root
    return lax.psum(jnp.where(mine, shard, jnp.zeros_like(shard)), axis)


def apply_map(extended, potential_in):
    inner_count = extended.shape[1] - 6
    width_y = extended.shape[2]
    width_z = extended.shape[3]
    padded = jnp.pad(extended, ((0, 0), (0, 0), (3, 3), (3, 3)))
    middle = padded[:, 3 : 3 + inner_count, 3 : 3 + width_y, 3 : 3 + width_z]
    laplace = 3.0 * stencil_taps[0] * middle
    for offset in (1, 2, 3):
        weight = stencil_taps[offset]
        laplace = laplace + weight * (
            padded[:, 3 + offset : 3 + offset + inner_count, 3 : 3 + width_y, 3 : 3 + width_z]
            + padded[:, 3 - offset : 3 - offset + inner_count, 3 : 3 + width_y, 3 : 3 + width_z]
        )
        laplace = laplace + weight * (
            padded[:, 3 : 3 + inner_count, 3 + offset : 3 + offset + width_y, 3 : 3 + width_z]
            + padded[:, 3 : 3 + inner_count, 3 - offset : 3 - offset + width_y, 3 : 3 + width_z]
        )
        laplace = laplace + weight * (
            padded[:, 3 : 3 + inner_count, 3 : 3 + width_y, 3 + offset : 3 + offset + width_z]
            + padded[:, 3 : 3 + inner_count, 3 : 3 + width_y, 3 - offset : 3 - offset + width_z]
        )
    energy = -0.5 * laplace + potential_in[None] * middle
    return (energy - center_shift * middle) * inverse_half


def coefficients(level_gap):
    ratio_q = (center_depth + level_gap) * inverse_half
    root_term = jnp.sqrt(ratio_q * ratio_q - 1.0)
    decay = ratio_q - root_term
    first = -inverse_half / root_term
    series = [first]
    current = first * (-2.0 * decay)
    series.append(current)
    for offset in range(2, SWEEPS + 1):
        current = current * -decay
        series.append(current)
    return [term[:, None, None, None] for term in series]


def sweep_single(initial, veff, series):
    summed = series[0] * initial
    previous = initial
    current = initial
    for offset in range(1, SWEEPS + 1):
        image = apply_map(extended_2(current, (("dom", 1),), 3), veff)
        if offset == 1:
            following = image
        else:
            following = 2.0 * image - previous
        summed = summed + series[offset] * following
        previous = current
        current = following
    return summed


def per_device(orbitals, veff, trials, owners, levels, shift_index):
    grid_cells = orbitals.shape[1] * orbitals.shape[2] * orbitals.shape[3] * lax.axis_size("dom")
    orbital_count = orbitals.shape[0] * lax.axis_size("orb")
    chosen = shift_index[:, None] == jnp.arange(levels.shape[0], dtype=jnp.int32)[None, :]
    level_gaps = jnp.sum(jnp.where(chosen, levels[None, :], 0.0), axis=1)
    series = coefficients(level_gaps)
    potentials = []
    for app_index in range(APPS):
        received = spread(trials[0], "orb", owners[app_index])
        trial_total = lax.psum(jnp.sum(received * received), "dom")
        potentials.append(received * lax.rsqrt(trial_total / grid_cells + norm_epsilon))
    responses = []
    for app_index in range(APPS):
        deltas = sweep_single(potentials[app_index][None] * orbitals, veff, series)
        local_sum = jnp.sum(orbitals * deltas, axis=0)
        responses.append(lax.psum(local_sum, "orb"))
    my_group = lax.axis_index("orb")
    result = jnp.zeros(orbitals.shape[1:], jnp.float32)
    for app_index in range(APPS):
        response = responses[app_index] * (4.0 / orbital_count)
        result = result + jnp.where(owners[app_index] == my_group, response, 0.0)
    return result[None]


def solution(mesh):
    placed = (
        P("orb", "dom", None, None),
        P("dom", None, None),
        P("orb", "dom", None, None),
        P(),
        P(),
        P("orb"),
    )
    return jax.shard_map(
        per_device,
        mesh=mesh,
        in_specs=placed,
        out_specs=P("orb", "dom", None, None),
        check_vma=False,
    )
```

profile of v0, /device:TPU:1, one launch (start us, length us, event | category | flops | bytes accessed | tf_op | source)
XLA Modules:
  0.0 520.6 jit_solution(1561641401315790378)
XLA Ops:
  9.2 1.8 select_bitcast_fusion.1
  12.0 120.3 %all-reduce.16.cloned.1.call-done = (f32[8,64,128]{2,1,0:T(8,128)}, f32[8,64,128]{2,1,0:T(8,128)}) async-done(((f32[8,64,128]{2,1,0:T(8,128)}, f32[8,64,128]{2,1,0:T(8,128)}), (f32[8,64,128]{2,1,0:T(8,128)}, f32[8,64,128]{2,1,0:T(8,128)})) %all-reduce.16.cloned.1.call-update) | async-done | bytes 524304 | tf_op jit(solution)/shard_map/psum | solution.py:32
  132.3 1.8 multiply_reduce_fusion
  134.1 20.7 %all-reduce.10 = (f32[]{:T(128)}, f32[]{:T(128)}) all-reduce(f32[]{:T(128)} %get-tuple-element.44, f32[]{:T(128)} %get-tuple-element.45), channel_id=1, replica_groups=mesh['orb'=16,'dom'=8] {'dom'}, use_global_device_ids=true, to_apply=%region_8.9 | all-reduce | flops 2 | bytes 16 | tf_op jit(solution)/shard_map/psum | solution.py:99
  160.4 4.0 collective-permute-start.1
  167.9 4.9 collective-permute-start.9
  172.8 2.7 collective-permute-done
  177.3 3.5 select_maximum_fusion.14
  180.8 10.7 %broadcast_multiply_fusion.2 = (f32[8,8,64,128]{3,2,1,0:T(8,128)S(1)}, f32[8,8,64,128]{3,2,1,0:T(8,128)}) fusion(f32[8,8,64,128]{3,2,1,0:T(8,128)} %copy-done.10, f32[8,64,128]{2,1,0:T(8,128)S(1)} %copy-done.11, f32[8,14,70,134]{3,2,1,0:T(8,128)S(1)} %select_maximum_fusion.14, f32[8,3,64,128]{3,2,1,0:T(8,128)} %copy-done.16, f32[8,3,64,128]{3,2,1,0:T(8,128)} %copy-done.14), kind=kLoop, calls=%fused_computation.397 | loop fusion | flops 20971520 | bytes 33292288 | tf_op jit(solution)/shard_map/mul | solution.py:57
  194.2 5.6 %collective-permute-start.3 = (f32[8,3,64,128]{3,2,1,0:T(8,128)}, f32[8,3,64,128]{3,2,1,0:T(8,128)}, u32[]{:S(2)}, u32[]{:S(2)}) collective-permute-start(f32[8,3,64,128]{3,2,1,0:T(8,128)} %get-tuple-element.25), channel_id=1, source_target_pairs={{0,1},{1,2},{2,3},{3,4},{4,5},{5,6},{6,7},{8,9},{9,10},{10,11},{11... | collective-permute-start | bytes 2359304 | tf_op jit(solution)/shard_map/ppermute | solution.py:22
  199.9 4.6 select_maximum_fusion.6
  204.5 10.6 %broadcast_multiply_fusion.1 = (f32[8,8,64,128]{3,2,1,0:T(8,128)S(1)}, f32[8,8,64,128]{3,2,1,0:T(8,128)}) fusion(f32[8,8,64,128]{3,2,1,0:T(8,128)} %copy-done.9, f32[8,64,128]{2,1,0:T(8,128)S(1)} %copy-done.11, f32[8,14,70,134]{3,2,1,0:T(8,128)S(1)} %select_maximum_fusion.6, f32[8,3,64,128]{3,2,1,0:T(8,128)} %collective-permute-done.9, ...), kind=kLoop, calls=%fused_computation.396 | loop fusion | flops 20971520 | bytes 33292288 | tf_op jit(solution)/shard_map/mul | solution.py:57
  217.9 5.0 collective-permute-start.11
  222.9 4.8 select_maximum_fusion.12
  227.7 9.5 %fusion.152 = f32[8,8,64,128]{3,2,1,0:T(8,128)S(1)} fusion(f32[8,8,64,128]{3,2,1,0:T(8,128)} %copy-done.4, f32[8,3,64,128]{3,2,1,0:T(8,128)} %collective-permute-done.3, f32[8,3,64,128]{3,2,1,0:T(8,128)} %collective-permute-done.2, f32[8,14,70,134]{3,2,1,0:T(8,128)S(1)} %select_maximum_fusion.12, f32[8,8,64,128]{3,2,1,0:T(8,128)S(1)} %copy-done.2, ...), kind=kLoop, calls=%fused_computation.236 | loop fusion | flops 22020096 | bytes 35651584 | tf_op jit(solution)/shard_map/sub | solution.py:83
  239.9 5.0 collective-permute-start.5
  244.9 4.8 select_maximum_fusion.4
  249.7 9.7 %fusion.63 = f32[8,8,64,128]{3,2,1,0:T(8,128)S(1)} fusion(f32[8,8,64,128]{3,2,1,0:T(8,128)} %copy-done.6, f32[8,3,64,128]{3,2,1,0:T(8,128)} %collective-permute-done.11, f32[8,3,64,128]{3,2,1,0:T(8,128)} %collective-permute-done.10, f32[8,14,70,134]{3,2,1,0:T(8,128)S(1)} %select_maximum_fusion.4, f32[8,8,64,128]{3,2,1,0:T(8,128)} %get-tuple-element.19, ...), kind=kLoop, calls=%fused_computation.147 | loop fusion | flops 22020096 | bytes 35651584 | tf_op jit(solution)/shard_map/sub | solution.py:83
  262.3 4.9 collective-permute-start.13
  267.2 4.5 select_maximum_fusion.10
  271.7 8.6 %fusion.130 = f32[8,8,64,128]{3,2,1,0:T(8,128)} fusion(f32[8,8,64,128]{3,2,1,0:T(8,128)S(1)} %fusion.152, f32[8,3,64,128]{3,2,1,0:T(8,128)} %collective-permute-done.5, f32[8,3,64,128]{3,2,1,0:T(8,128)S(1)} %collective-permute-done.4, f32[8,14,70,134]{3,2,1,0:T(8,128)S(1)} %select_maximum_fusion.10, f32[8,64,128]{2,1,0:T(8,128)S(1)} %copy-done.11, ...), kind=kLoop, calls=%fused_computation.214 | loop fusion | flops 22020096 | bytes 33292288 | tf_op jit(solution)/shard_map/sub | solution.py:83
  280.3 2.7 fusion.251
  284.3 7.1 %collective-permute-start.7 = (f32[8,3,64,128]{3,2,1,0:T(8,128)}, f32[8,3,64,128]{3,2,1,0:T(8,128)}, u32[]{:S(2)}, u32[]{:S(2)}) collective-permute-start(f32[8,3,64,128]{3,2,1,0:T(8,128)} %get-tuple-element.20), channel_id=1, source_target_pairs={{0,1},{1,2},{2,3},{3,4},{4,5},{5,6},{6,7},{8,9},{9,10},{10,11},{11... | collective-permute-start | bytes 2359304 | tf_op jit(solution)/shard_map/ppermute | solution.py:22
  291.4 4.8 select_maximum_fusion.2
  296.2 8.8 %fusion.41 = f32[8,8,64,128]{3,2,1,0:T(8,128)} fusion(f32[8,8,64,128]{3,2,1,0:T(8,128)S(1)} %fusion.63, f32[8,3,64,128]{3,2,1,0:T(8,128)} %collective-permute-done.13, f32[8,3,64,128]{3,2,1,0:T(8,128)} %collective-permute-done.12, f32[8,14,70,134]{3,2,1,0:T(8,128)S(1)} %select_maximum_fusion.2, f32[8,64,128]{2,1,0:T(8,128)S(1)} %copy-done.11, ...), kind=kLoop, calls=%fused_computation.125 | loop fusion | flops 22020096 | bytes 33292288 | tf_op jit(solution)/shard_map/sub | solution.py:83
  308.0 7.1 %collective-permute-start.15 = (f32[8,3,64,128]{3,2,1,0:T(8,128)S(1)}, f32[8,3,64,128]{3,2,1,0:T(8,128)S(1)}, u32[]{:S(2)}, u32[]{:S(2)}) collective-permute-start(f32[8,3,64,128]{3,2,1,0:T(8,128)S(1)} %get-tuple-element.30), channel_id=1, source_target_pairs={{0,1},{1,2},{2,3},{3,4},{4,5},{5,6},{6,7},{8,9},{9,10},{10,11},{11... | collective-permute-start | bytes 2359304 | tf_op jit(solution)/shard_map/ppermute | solution.py:22
  315.1 6.6 %select_maximum_fusion.8 = f32[8,14,70,134]{3,2,1,0:T(8,128)} fusion(f32[8,3,64,128]{3,2,1,0:T(8,128)S(1)} %collective-permute-done.6, f32[8,8,64,128]{3,2,1,0:T(8,128)S(1)} %copy-done.3, f32[8,3,64,128]{3,2,1,0:T(8,128)} %collective-permute-done.7), kind=kLoop, calls=%fused_computation.12 | loop fusion | flops 15758400 | bytes 7872256 | tf_op jit(solution)/shard_map/concatenate | solution.py:26
  323.8 3.5 select_maximum_fusion
  327.3 28.0 %fusion.245 = f32[8,64,128]{2,1,0:T(8,128)} fusion(f32[8,8,64,128]{3,2,1,0:T(8,128)S(1)} %copy-done, f32[8,8,64,128]{3,2,1,0:T(8,128)S(1)} %fusion.152, f32[8,8,64,128]{3,2,1,0:T(8,128)} %fusion.130, f32[8,14,70,134]{3,2,1,0:T(8,128)} %select_maximum_fusion.8, f32[8,3,64,128]{3,2,1,0:T(8,128)} %collective-permute-done.7, f32[8,3,64,128]{3,2,1,0:T(8,128)} %copy-done.13, ...), kind=kLoop, calls=%fused_computation.393 | loop fusion | flops 27721728 | bytes 35913888 | tf_op jit(solution)/shard_map/reduce_sum | solution.py:104
  355.3 11.3 %fusion.246 = f32[8,64,128]{2,1,0:T(8,128)} fusion(f32[8,8,64,128]{3,2,1,0:T(8,128)S(1)} %copy-done, f32[8,8,64,128]{3,2,1,0:T(8,128)} %copy-done.1, f32[8,8,64,128]{3,2,1,0:T(8,128)} %fusion.41, f32[8,14,70,134]{3,2,1,0:T(8,128)S(1)} %select_maximum_fusion, f32[8,3,64,128]{3,2,1,0:T(8,128)} %copy-done.17, f32[8,3,64,128]{3,2,1,0:T(8,128)} %copy-done.15, ...), kind=kLoop, calls=%fused_computation.394 | loop fusion | flops 27721728 | bytes 35913888 | tf_op jit(solution)/shard_map/reduce_sum | solution.py:104
  367.9 144.0 %all-reduce.14.cloned.1.call-done = (f32[8,64,128]{2,1,0:T(8,128)}, f32[8,64,128]{2,1,0:T(8,128)}) async-done(((f32[8,64,128]{2,1,0:T(8,128)}, f32[8,64,128]{2,1,0:T(8,128)}), (f32[8,64,128]{2,1,0:T(8,128)}, f32[8,64,128]{2,1,0:T(8,128)})) %all-reduce.14.cloned.1.call-update) | async-done | bytes 524304 | tf_op jit(solution)/shard_map/psum | solution.py:105
  511.9 1.8 add_bitcast_fusion
  (80 shorter events, 29.1 us)
Async XLA Ops:
  6.5 151.6 %copy-start = (f32[8,8,64,128]{3,2,1,0:T(8,128)S(1)}, f32[8,8,64,128]{3,2,1,0:T(8,128)}, u32[]{:S(2)}) copy-start(f32[8,8,64,128]{3,2,1,0:T(8,128)} %param.6) | copy-start | bytes 6291460
  6.5 125.8 %all-reduce.16.cloned.1.call-start = ((), (), s32[]{:S(2)}) async-start(), calls=%async_computation.1 | async-start | bytes 1048576 | tf_op jit(solution)/shard_map/psum | solution.py:32
  11.1 500.9 %all-reduce.14.cloned.1.call-start = ((), (), s32[]{:S(2)}) async-start(), calls=%async_computation | async-start | bytes 1048576 | tf_op jit(solution)/shard_map/psum | solution.py:105
  158.9 17.6 %copy-start.10 = (f32[8,8,64,128]{3,2,1,0:T(8,128)}, f32[8,8,64,128]{3,2,1,0:T(8,128)S(1)}, u32[]{:S(2)}) copy-start(f32[8,8,64,128]{3,2,1,0:T(8,128)S(1)} %get-tuple-element.28) | copy-start | bytes 6291460
  158.9 41.0 %copy-start.9 = (f32[8,8,64,128]{3,2,1,0:T(8,128)}, f32[8,8,64,128]{3,2,1,0:T(8,128)S(1)}, u32[]{:S(2)}) copy-start(f32[8,8,64,128]{3,2,1,0:T(8,128)S(1)} %get-tuple-element.29) | copy-start | bytes 6291460
  158.9 5.6 %copy-start.11 = (f32[8,64,128]{2,1,0:T(8,128)S(1)}, f32[8,64,128]{2,1,0:T(8,128)}, u32[]{:S(2)}) copy-start(f32[8,64,128]{2,1,0:T(8,128)} %param.7) | copy-start | bytes 786436
  159.0 16.6 %collective-permute-start = (f32[8,3,64,128]{3,2,1,0:T(8,128)S(1)}, f32[8,3,64,128]{3,2,1,0:T(8,128)S(1)}, u32[]{:S(2)}, u32[]{:S(2)}) collective-permute-start(f32[8,3,64,128]{3,2,1,0:T(8,128)S(1)} %get-tuple-element.27), channel_id=1, source_target_pairs={{1,0},{2,1},{3,2},{4,3},{5,4},{6,5},{7,6},{9,8},{10,9},{11,10},{12... | collective-permute-start | bytes 2359304 | tf_op jit(solution)/shard_map/ppermute | solution.py:25
  160.4 16.0 %collective-permute-start.1 = (f32[8,3,64,128]{3,2,1,0:T(8,128)S(1)}, f32[8,3,64,128]{3,2,1,0:T(8,128)S(1)}, u32[]{:S(2)}, u32[]{:S(2)}) collective-permute-start(f32[8,3,64,128]{3,2,1,0:T(8,128)S(1)} %get-tuple-element.26), channel_id=1, source_target_pairs={{0,1},{1,2},{2,3},{3,4},{4,5},{5,6},{6,7},{8,9},{9,10},{10,11},{11... | collective-permute-start | bytes 2359304 | tf_op jit(solution)/shard_map/ppermute | solution.py:22
  166.6 33.3 %collective-permute-start.8 = (f32[8,3,64,128]{3,2,1,0:T(8,128)}, f32[8,3,64,128]{3,2,1,0:T(8,128)S(1)}, u32[]{:S(2)}, u32[]{:S(2)}) collective-permute-start(f32[8,3,64,128]{3,2,1,0:T(8,128)} %get-tuple-element.37), channel_id=1, source_target_pairs={{1,0},{2,1},{3,2},{4,3},{5,4},{6,5},{7,6},{9,8},{10,9},{11,10},{12... | collective-permute-start | bytes 2359304 | tf_op jit(solution)/shard_map/ppermute | solution.py:25
  167.9 32.0 %collective-permute-start.9 = (f32[8,3,64,128]{3,2,1,0:T(8,128)}, f32[8,3,64,128]{3,2,1,0:T(8,128)}, u32[]{:S(2)}, u32[]{:S(2)}) collective-permute-start(f32[8,3,64,128]{3,2,1,0:T(8,128)} %get-tuple-element.36), channel_id=1, source_target_pairs={{0,1},{1,2},{2,3},{3,4},{4,5},{5,6},{6,7},{8,9},{9,10},{10,11},{11... | collective-permute-start | bytes 2359304 | tf_op jit(solution)/shard_map/ppermute | solution.py:22
  191.5 13.0 %copy-start.4 = (f32[8,8,64,128]{3,2,1,0:T(8,128)}, f32[8,8,64,128]{3,2,1,0:T(8,128)S(1)}, u32[]{:S(2)}) copy-start(f32[8,8,64,128]{3,2,1,0:T(8,128)S(1)} %get-tuple-element.11) | copy-start | bytes 6291460
  193.0 29.9 %collective-permute-start.2 = (f32[8,3,64,128]{3,2,1,0:T(8,128)}, f32[8,3,64,128]{3,2,1,0:T(8,128)}, u32[]{:S(2)}, u32[]{:S(2)}) collective-permute-start(f32[8,3,64,128]{3,2,1,0:T(8,128)} %get-tuple-element.24), channel_id=1, source_target_pairs={{1,0},{2,1},{3,2},{4,3},{5,4},{6,5},{7,6},{9,8},{10,9},{11,10},{12... | collective-permute-start | bytes 2359304 | tf_op jit(solution)/shard_map/ppermute | solution.py:25
  194.2 28.7 %collective-permute-start.3 = (f32[8,3,64,128]{3,2,1,0:T(8,128)}, f32[8,3,64,128]{3,2,1,0:T(8,128)}, u32[]{:S(2)}, u32[]{:S(2)}) collective-permute-start(f32[8,3,64,128]{3,2,1,0:T(8,128)} %get-tuple-element.25), channel_id=1, source_target_pairs={{0,1},{1,2},{2,3},{3,4},{4,5},{5,6},{6,7},{8,9},{9,10},{10,11},{11... | collective-permute-start | bytes 2359304 | tf_op jit(solution)/shard_map/ppermute | solution.py:22
  215.1 7.8 %copy-start.6 = (f32[8,8,64,128]{3,2,1,0:T(8,128)}, f32[8,8,64,128]{3,2,1,0:T(8,128)S(1)}, u32[]{:S(2)}) copy-start(f32[8,8,64,128]{3,2,1,0:T(8,128)S(1)} %get-tuple-element.18) | copy-start | bytes 6291460
  215.1 7.8 %copy-start.5 = (f32[8,8,64,128]{3,2,1,0:T(8,128)S(1)}, f32[8,8,64,128]{3,2,1,0:T(8,128)}, u32[]{:S(2)}) copy-start(f32[8,8,64,128]{3,2,1,0:T(8,128)} %copy-done.4) | copy-start | bytes 6291460
  216.4 28.5 %collective-permute-start.10 = (f32[8,3,64,128]{3,2,1,0:T(8,128)}, f32[8,3,64,128]{3,2,1,0:T(8,128)}, u32[]{:S(2)}, u32[]{:S(2)}) collective-permute-start(f32[8,3,64,128]{3,2,1,0:T(8,128)} %get-tuple-element.34), channel_id=1, source_target_pairs={{1,0},{2,1},{3,2},{4,3},{5,4},{6,5},{7,6},{9,8},{10,9},{11,10},{12... | collective-permute-start | bytes 2359304 | tf_op jit(solution)/shard_map/ppermute | solution.py:25
  217.8 9.9 %copy-start.2 = (f32[8,8,64,128]{3,2,1,0:T(8,128)S(1)}, f32[8,8,64,128]{3,2,1,0:T(8,128)}, u32[]{:S(2)}) copy-start(f32[8,8,64,128]{3,2,1,0:T(8,128)} %get-tuple-element.12) | copy-start | bytes 6291460
  217.9 27.0 %collective-permute-start.11 = (f32[8,3,64,128]{3,2,1,0:T(8,128)}, f32[8,3,64,128]{3,2,1,0:T(8,128)}, u32[]{:S(2)}, u32[]{:S(2)}) collective-permute-start(f32[8,3,64,128]{3,2,1,0:T(8,128)} %get-tuple-element.35), channel_id=1, source_target_pairs={{0,1},{1,2},{2,3},{3,4},{4,5},{5,6},{6,7},{8,9},{9,10},{10,11},{11... | collective-permute-start | bytes 2359304 | tf_op jit(solution)/shard_map/ppermute | solution.py:22
  237.2 7.7 %copy-start.7 = (f32[8,8,64,128]{3,2,1,0:T(8,128)S(1)}, f32[8,8,64,128]{3,2,1,0:T(8,128)}, u32[]{:S(2)}) copy-start(f32[8,8,64,128]{3,2,1,0:T(8,128)} %copy-done.6) | copy-start | bytes 6291460
  238.6 28.6 %collective-permute-start.4 = (f32[8,3,64,128]{3,2,1,0:T(8,128)}, f32[8,3,64,128]{3,2,1,0:T(8,128)S(1)}, u32[]{:S(2)}, u32[]{:S(2)}) collective-permute-start(f32[8,3,64,128]{3,2,1,0:T(8,128)} %get-tuple-element.22), channel_id=1, source_target_pairs={{1,0},{2,1},{3,2},{4,3},{5,4},{6,5},{7,6},{9,8},{10,9},{11,10},{12... | collective-permute-start | bytes 2359304 | tf_op jit(solution)/shard_map/ppermute | solution.py:25
  239.9 9.8 %copy-start.18 = (f32[8,64,128]{2,1,0:T(8,128)S(1)}, f32[8,64,128]{2,1,0:T(8,128)}, u32[]{:S(2)}) copy-start(f32[8,64,128]{2,1,0:T(8,128)} %broadcast_multiply_fusion.5) | copy-start | bytes 786436
  239.9 27.3 %collective-permute-start.5 = (f32[8,3,64,128]{3,2,1,0:T(8,128)}, f32[8,3,64,128]{3,2,1,0:T(8,128)}, u32[]{:S(2)}, u32[]{:S(2)}) collective-permute-start(f32[8,3,64,128]{3,2,1,0:T(8,128)} %get-tuple-element.23), channel_id=1, source_target_pairs={{0,1},{1,2},{2,3},{3,4},{4,5},{5,6},{6,7},{8,9},{9,10},{10,11},{11... | collective-permute-start | bytes 2359304 | tf_op jit(solution)/shard_map/ppermute | solution.py:22
  259.4 36.7 %copy-start.1 = (f32[8,8,64,128]{3,2,1,0:T(8,128)}, f32[8,8,64,128]{3,2,1,0:T(8,128)S(1)}, u32[]{:S(2)}) copy-start(f32[8,8,64,128]{3,2,1,0:T(8,128)S(1)} %fusion.63) | copy-start | bytes 6291460
  261.0 30.4 %collective-permute-start.12 = (f32[8,3,64,128]{3,2,1,0:T(8,128)}, f32[8,3,64,128]{3,2,1,0:T(8,128)}, u32[]{:S(2)}, u32[]{:S(2)}) collective-permute-start(f32[8,3,64,128]{3,2,1,0:T(8,128)} %get-tuple-element.32), channel_id=1, source_target_pairs={{1,0},{2,1},{3,2},{4,3},{5,4},{6,5},{7,6},{9,8},{10,9},{11,10},{12... | collective-permute-start | bytes 2359304 | tf_op jit(solution)/shard_map/ppermute | solution.py:25
  262.3 29.1 %collective-permute-start.13 = (f32[8,3,64,128]{3,2,1,0:T(8,128)}, f32[8,3,64,128]{3,2,1,0:T(8,128)}, u32[]{:S(2)}, u32[]{:S(2)}) collective-permute-start(f32[8,3,64,128]{3,2,1,0:T(8,128)} %get-tuple-element.33), channel_id=1, source_target_pairs={{0,1},{1,2},{2,3},{3,4},{4,5},{5,6},{6,7},{8,9},{9,10},{10,11},{11... | collective-permute-start | bytes 2359304 | tf_op jit(solution)/shard_map/ppermute | solution.py:22
  283.0 32.1 %collective-permute-start.6 = (f32[8,3,64,128]{3,2,1,0:T(8,128)}, f32[8,3,64,128]{3,2,1,0:T(8,128)S(1)}, u32[]{:S(2)}, u32[]{:S(2)}) collective-permute-start(f32[8,3,64,128]{3,2,1,0:T(8,128)} %get-tuple-element.21), channel_id=1, source_target_pairs={{1,0},{2,1},{3,2},{4,3},{5,4},{6,5},{7,6},{9,8},{10,9},{11,10},{12... | collective-permute-start | bytes 2359304 | tf_op jit(solution)/shard_map/ppermute | solution.py:25
  284.3 30.8 %collective-permute-start.7 = (f32[8,3,64,128]{3,2,1,0:T(8,128)}, f32[8,3,64,128]{3,2,1,0:T(8,128)}, u32[]{:S(2)}, u32[]{:S(2)}) collective-permute-start(f32[8,3,64,128]{3,2,1,0:T(8,128)} %get-tuple-element.20), channel_id=1, source_target_pairs={{0,1},{1,2},{2,3},{3,4},{4,5},{5,6},{6,7},{8,9},{9,10},{10,11},{11... | collective-permute-start | bytes 2359304 | tf_op jit(solution)/shard_map/ppermute | solution.py:22
  305.0 10.2 %copy-start.3 = (f32[8,8,64,128]{3,2,1,0:T(8,128)S(1)}, f32[8,8,64,128]{3,2,1,0:T(8,128)}, u32[]{:S(2)}) copy-start(f32[8,8,64,128]{3,2,1,0:T(8,128)} %fusion.130) | copy-start | bytes 6291460
  306.7 15.5 %collective-permute-start.14 = (f32[8,3,64,128]{3,2,1,0:T(8,128)S(1)}, f32[8,3,64,128]{3,2,1,0:T(8,128)S(1)}, u32[]{:S(2)}, u32[]{:S(2)}) collective-permute-start(f32[8,3,64,128]{3,2,1,0:T(8,128)S(1)} %get-tuple-element.31), channel_id=1, source_target_pairs={{1,0},{2,1},{3,2},{4,3},{5,4},{6,5},{7,6},{9,8},{10,9},{11,10},{12... | collective-permute-start | bytes 2359304 | tf_op jit(solution)/shard_map/ppermute | solution.py:25
  308.0 15.8 %copy-start.8 = (f32[8,8,64,128]{3,2,1,0:T(8,128)S(1)}, f32[8,8,64,128]{3,2,1,0:T(8,128)}, u32[]{:S(2)}) copy-start(f32[8,8,64,128]{3,2,1,0:T(8,128)} %fusion.41) | copy-start | bytes 6291460
  308.0 15.8 %collective-permute-start.15 = (f32[8,3,64,128]{3,2,1,0:T(8,128)S(1)}, f32[8,3,64,128]{3,2,1,0:T(8,128)S(1)}, u32[]{:S(2)}, u32[]{:S(2)}) collective-permute-start(f32[8,3,64,128]{3,2,1,0:T(8,128)S(1)} %get-tuple-element.30), channel_id=1, source_target_pairs={{0,1},{1,2},{2,3},{3,4},{4,5},{5,6},{6,7},{8,9},{9,10},{10,11},{11... | collective-permute-start | bytes 2359304 | tf_op jit(solution)/shard_map/ppermute | solution.py:22
  315.1 6.7 %copy-start.13 = (f32[8,3,64,128]{3,2,1,0:T(8,128)}, f32[8,3,64,128]{3,2,1,0:T(8,128)S(1)}, u32[]{:S(2)}) copy-start(f32[8,3,64,128]{3,2,1,0:T(8,128)S(1)} %collective-permute-done.6) | copy-start | bytes 2359300
  (5 other events, 11.2 us)
Sparse Core Ops, SparseCore 0:
  11.2 121.0 all-reduce.15
  366.8 145.1 all-reduce.13
where the time goes:
time: 522 us; the launch traced here: 521 us
  waiting for transfers between devices  270 us (52%)
  other arithmetic  144 us (28%)
  starting transfers between devices  54.3 us (10%)
  blocking collectives  20.7 us (4%)
  between operations  17.7 us (3%)
  local copies, waits for them, and re-layouts  14.1 us (3%)
    psum x1, waiting for transfers between devices, per_device(): responses.append(lax.psum(local_sum, 'orb'))  144 us
    psum x1, waiting for transfers between devices, spread(): return lax.psum(jnp.where(mine, shard, jnp.zeros_like(shard)), axis)  120 us
    ppermute x8, starting transfers between devices, extended_2(): lax.ppermute(lax.slice_in_dim(block, block.shape[dim] - width, None, axis...  43.7 us
    reduce_sum x2, other arithmetic, per_device(): local_sum = jnp.sum(orbitals * deltas, axis=0)  39.4 us
    concatenate x8, other arithmetic, extended_2(): block = jnp.concatenate([low, block, high], axis=dim)  37.1 us
    sub x4, other arithmetic, sweep_single(): following = 2.0 * image - previous  36.6 us
    mul x2, other arithmetic, apply_map(): return (energy - center_shift * middle) * inverse_half  21.3 us
    psum x1, blocking collectives, per_device(): trial_total = lax.psum(jnp.sum(received * received), 'dom')  20.7 us
  transfers between devices with their start and end apart: 18, of which 6 were waited for; matrix products, arithmetic and copies ran while one was open for 20% of the time, Pallas kernels for 0%

commit v1 on v0

v1 whole, which is shorter than its diff:
```python
import functools

import jax
import jax.numpy as jnp
import numpy as np
from jax import lax
from jax.experimental import pallas as pl
from jax.experimental.pallas import tpu as pltpu
from jax.sharding import PartitionSpec as P

APPS = 2
SWEEPS = 4
MESH = pl.DeviceIdType.MESH

taps = (135.0, -13.5, 1.0)
inverse_half = 1.0 / 5.05
center_depth = 5.05
norm_epsilon = 1e-06
beta = -0.5 * inverse_half / 90.0
center_rest = 49.0 / 12.0 - 4.05

XP, YP, ZP = 2, 1, 0
GROUPS = ((0, 24), (24, 24), (48, 16))


def place():
    orb, dom = lax.axis_index("orb"), lax.axis_index("dom")
    return dom % 4, dom // 4, orb // 8, (orb // 2) % 4, orb % 2


def device(x, y, z, c):
    return ((y % 2) * 8 + z * 2 + c, (y // 2) * 4 + x)


class Copies:
    def __init__(self, send, recv):
        self.send, self.recv, self.count = send, recv, 0

    def remote(self, src, dst, target):
        at = self.count
        self.count += 1
        copy = pltpu.make_async_remote_copy(
            src_ref=src,
            dst_ref=dst,
            send_sem=self.send.at[at],
            recv_sem=self.recv.at[at],
            device_id=target,
            device_id_type=MESH,
        )
        copy.start()
        return copy

    def local(self, src, dst):
        at = self.count
        self.count += 1
        copy = pltpu.make_async_copy(src, dst, self.send.at[at])
        copy.start()
        return copy


SEMS = 160


def kernel(
    orbitals, veff, trials, table, band, out,
    phi, vfull, geff, masked, scattered, coef, fields, work_a, work_b, resp,
    r0a, r1a, r2a, r0b, r1b, r2b, r0c, r1c, r2c, s0a, s1a, s2a, s0b, s1b, s2b, final, slabs,
    send, recv,
):
    x, yh, yl, z, c = place()
    y = 2 * yh + yl
    orb, dom = lax.axis_index("orb"), lax.axis_index("dom")
    own = yl * 4 + z
    copies = Copies(send, recv)

    def along(dim, r):
        if dim == XP:
            return device((x + r) % 4, y, z, c)
        if dim == YP:
            return device(x, (y + r) % 4, z, c)
        return device(x, y, (z + r) % 4, c)

    sibling = device(x, y, z, 1 - c)

    barrier = pltpu.get_barrier_semaphore()
    peers = [((orb + r) % 16, dom) for r in range(1, 16)]
    peers += [(orb, (dom + r) % 8) for r in range(1, 8)]
    peers += [along(YP, 1), along(YP, 3)]
    for peer in peers:
        pl.semaphore_signal(barrier, inc=1, device_id=peer, device_id_type=MESH)
    pl.semaphore_wait(barrier, len(peers))

    for app in range(APPS):
        for i in range(8):
            masked[app, i] = trials[0, i] * table[8, app : app + 1, :]
    spread = []
    for r in range(1, 16):
        to = (orb + r) % 16
        spread.append(copies.remote(masked.at[to % 2, to // 2], scattered.at[orb], (to, dom)))
    half = pl.ds(c * 32, 32)
    piece = veff.at[own, half]
    veff_x = [copies.remote(piece, geff.at[yh, x, yl, z, half], along(XP, r)) for r in (1, 3, 2)]
    veff_own = copies.local(piece, geff.at[yh, x, yl, z, half])
    moved = []
    for r in (4, 6, 5, 7, 2, 1, 3):
        to = (dom + r) % 8
        moved.append((r, copies.remote(orbitals.at[to], phi.at[c, dom], (orb, to))))
    phi_own = copies.local(orbitals.at[dom], phi.at[c, dom])
    phi_pair = [copies.remote(orbitals.at[dom], phi.at[c, dom], sibling)]
    coef_own = copies.local(table.at[dom], coef.at[c])
    coef_pair = copies.remote(table.at[dom], coef.at[c], sibling)

    zero_rows = jnp.zeros((8, 128), jnp.float32)
    zero_plane = jnp.zeros((80, 128), jnp.float32)
    for buffer in (fields, work_a, work_b):
        for k in range(2):
            for p in (0, 1, 2, 67, 68, 69):
                buffer[k, p] = zero_plane

            def border(p, carry, buffer=buffer, k=k):
                buffer[k, p, 0:8] = zero_rows
                buffer[k, p, 72:80] = zero_rows
                return carry

            lax.fori_loop(3, 67, border, 0)

    scattered[orb] = masked[c, own]
    for copy in spread:
        copy.wait()
    total = scattered[0]
    for g in range(1, 16):
        total = total + scattered[g]
    vfull[yh, x, yl, z] = total
    v_x = [copies.remote(vfull.at[yh, x, yl, z], vfull.at[yh, x, yl, z], along(XP, r)) for r in (1, 3, 2)]

    veff_own.wait()
    for copy in veff_x:
        copy.wait()
    row = geff.at[yh, :, yl, z, half]
    veff_y = [copies.remote(row, row, along(YP, r)) for r in (1, 3, 2)]
    for copy in v_x:
        copy.wait()
    row = vfull.at[yh, :, yl, z]
    v_y = [copies.remote(row, row, along(YP, r)) for r in (1, 3, 2)]
    for copy in veff_y:
        copy.wait()
    pairs = []

    def ring(at):
        block = at(z, None)
        return [copies.remote(block, block, along(ZP, r)) for r in (1, 3)]

    def relay(at, sends):
        for copy in sends:
            copy.wait()
        first, second = at((z + 3) % 4, 0), at((z + 1) % 4, 1)
        return [copies.remote(first, first, along(ZP, 1)), copies.remote(second, second, along(ZP, 3))]

    def at_g(zz, part):
        if part is None:
            return geff.at[:, :, :, zz, half]
        return geff.at[part, :, :, zz, half]

    def at_v(zz, part):
        if part is None:
            return vfull.at[:, :, :, zz]
        return vfull.at[part, :, :, zz]

    g_z = ring(at_g)
    for copy in v_y:
        copy.wait()
    v_z = ring(at_v)
    g_r = relay(at_g, g_z)
    v_r = relay(at_v, v_z)

    phi_own.wait()
    for r, copy in moved:
        copy.wait()
        source = phi.at[c, (dom - r + 8) % 8]
        phi_pair.append(copies.remote(source, source, sibling))
    for copy in g_r:
        copy.wait()
    everything = geff.at[:, :, :, :, half]
    g_pair = copies.remote(everything, everything, sibling)
    for copy in v_r:
        copy.wait()
    for copy in phi_pair:
        copy.wait()
    coef_own.wait()
    coef_pair.wait()
    g_pair.wait()

    def start(p, norm):
        h, a, b, d = p // 32, (p // 8) % 4, (p // 4) % 2, p % 4
        v = vfull[h, a, b, d]
        for k in range(2):
            fields[k, p + 3, 8:72] = v * phi[k, p // 8, p % 8]
        geff[h, a, b, d] = (geff[h, a, b, d] + center_rest) * -180.0
        sq = v * v
        return norm + jnp.sum(sq.reshape(8, 8, 128), axis=0)

    norm = lax.fori_loop(0, 64, start, jnp.zeros((8, 128), jnp.float32))
    scale = lax.rsqrt(jnp.sum(norm, keepdims=True) * (1.0 / 524288) + norm_epsilon)

    def image(src, p, step):
        h, a, b, d = p // 32, (p // 8) % 4, (p // 4) % 2, p % 4
        both = jnp.concatenate([src[0, p + 3, 8:72], src[1, p + 3, 8:72]], axis=0)
        high = both.astype(jnp.bfloat16)
        low = (both - high.astype(jnp.float32)).astype(jnp.bfloat16)
        along_z = jnp.dot(
            jnp.concatenate([high, low], axis=1), band[...], preferred_element_type=jnp.float32
        )
        g = geff[h, a, b, d]
        results = []
        for k in range(2):
            acc = along_z[k * 64 : k * 64 + 64] + g * src[k, p + 3, 8:72]
            acc = acc + coef[k, step : step + 1, :] * fields[k, p + 3, 8:72]
            for j in (1, 2, 3):
                near = (src[k, p + 3 + j, 8:72] + src[k, p + 3 - j, 8:72]) + (
                    src[k, p + 3, 8 + j : 72 + j] + src[k, p + 3, 8 - j : 72 - j]
                )
                acc = acc + (near if j == 3 else near * taps[j - 1])
            results.append(acc)
        return results

    for step, (src, dst) in enumerate(((fields, work_a), (work_a, work_b), (work_b, work_a))):

        def sweep(p, carry, step=step, src=src, dst=dst):
            for k, value in enumerate(image(src, p, step)):
                dst[k, p + 3, 8:72] = value
            return carry

        lax.fori_loop(0, 64, sweep, 0)

    gain = [scale * coef[k, 4:5, :] for k in range(2)]

    def last(p, carry):
        h, a, b, d = p // 32, (p // 8) % 4, (p // 4) % 2, p % 4
        one, two = image(work_a, p, 3)
        resp[h, a, b, d] = one * (gain[0] * phi[0, p // 8, p % 8]) + two * (gain[1] * phi[1, p // 8, p % 8])
        return carry

    lax.fori_loop(0, 64, last, 0)

    def part(dim, r, ref, kept):
        if dim == XP:
            to = (x + r) % 4
            where = {"x": to}
        elif dim == YP:
            to = (y + r) % 4
            where = {"yh": to // 2, "yl": to % 2}
        else:
            where = {"z": (z + r) % 4}
        return ref.at[tuple(where.get(name, slice(None)) for name in kept)]

    names = {XP: ("x",), YP: ("yh", "yl"), ZP: ("z",)}
    orders = ((ZP, YP, XP), (YP, XP, ZP), (XP, ZP, YP))
    stages = ((r0a, r1a, r2a), (r0b, r1b, r2b), (r0c, r1c, r2c))
    sums = ((s0a, s1a, s2a), (s0b, s1b, s2b))
    kept = [("yh", "x", "yl", "z") for _ in GROUPS]
    current = [resp.at[:, :, :, :, first : first + count] for first, count in GROUPS]
    for stage in range(3):
        started = []
        for q in range(3):
            dim = orders[q][stage]
            started.append(
                [
                    copies.remote(part(dim, r, current[q], kept[q]), stages[stage][q].at[r - 1], along(dim, r))
                    for r in (1, 3, 2)
                ]
            )
        for q in range(3):
            dim = orders[q][stage]
            for copy in started[q]:
                copy.wait()
            received = stages[stage][q]
            mine = part(dim, 0, current[q], kept[q])
            kept[q] = tuple(name for name in kept[q] if name not in names[dim])
            first, count = GROUPS[q]
            if stage == 2:
                final[first : first + count] = (mine[...] + received[0]) + (received[1] + received[2])
            else:
                sums[stage][q][...] = (mine[...] + received[0]) + (received[1] + received[2])
                current[q] = sums[stage][q]

    slabs[c, own] = final[...]
    shared = []
    for r in range(1, 16):
        to = (orb + r) % 16
        shared.append(copies.remote(final, slabs.at[c, own], (to, dom)))
    for copy in shared:
        copy.wait()
    for i in range(8):
        out[0, i] = slabs[0, i] * table[8, 0:1, :] + slabs[1, i] * table[8, 1:2, :]


def coefficients(level_gap, orbital_count):
    ratio_q = (center_depth + level_gap) * inverse_half
    root_term = jnp.sqrt(ratio_q * ratio_q - 1.0)
    decay = ratio_q - root_term
    c0 = -inverse_half / root_term
    c1 = c0 * (-2.0 * decay)
    c2 = c1 * -decay
    c3 = c2 * -decay
    c4 = c3 * -decay
    d0, d1, d2, d3, d4 = c0 - c2 + c4, c1 - 3.0 * c3, 2.0 * c2 - 8.0 * c4, 4.0 * c3, 8.0 * c4
    inverse = 1.0 / d4
    zero = jnp.zeros_like(d0)
    rows = [
        d3 * inverse * (1.0 / beta),
        d2 * inverse * (1.0 / beta**2),
        d1 * inverse * (1.0 / beta**3),
        d0 * inverse * (1.0 / beta**4),
        d4 * (beta**4 * 4.0 / orbital_count),
        zero,
        zero,
        zero,
    ]
    return jnp.stack(rows, axis=1)


def band_matrix():
    d = np.zeros((128, 128), np.float32)
    for j, tap in enumerate(taps, 1):
        d += tap * (np.eye(128, k=j) + np.eye(128, k=-j))
    return np.concatenate([d, d], axis=0)


def per_device(orbitals, veff, trials, owners, levels, shift_index):
    orbital_count = orbitals.shape[0] * lax.axis_size("orb")
    chosen = shift_index[:, None] == jnp.arange(levels.shape[0], dtype=jnp.int32)[None, :]
    level_gaps = jnp.sum(jnp.where(chosen, levels[None, :], 0.0), axis=1)
    masks = (owners == lax.axis_index("orb")).astype(jnp.float32)
    masks = jnp.concatenate([masks, jnp.zeros((6,), jnp.float32)])
    table = jnp.concatenate([coefficients(level_gaps, orbital_count), masks[None]], axis=0)
    table = jnp.broadcast_to(table[:, :, None], (9, 8, 128))
    band = jnp.asarray(band_matrix(), jnp.bfloat16)
    f32 = jnp.float32
    vm = lambda *shape: pltpu.VMEM(shape, f32)
    full = (2, 4, 2, 4, 64, 128)
    return pl.pallas_call(
        kernel,
        out_shape=jax.ShapeDtypeStruct((1, 8, 64, 128), f32),
        in_specs=[
            pl.BlockSpec(memory_space=pl.ANY),
            pl.BlockSpec(memory_space=pl.ANY),
            pl.BlockSpec(memory_space=pltpu.VMEM),
            pl.BlockSpec(memory_space=pltpu.VMEM),
            pl.BlockSpec(memory_space=pltpu.VMEM),
        ],
        out_specs=pl.BlockSpec(memory_space=pltpu.VMEM),
        scratch_shapes=[
            vm(2, 8, 8, 64, 128),
            vm(*full),
            vm(*full),
            vm(2, 8, 64, 128),
            vm(16, 64, 128),
            vm(2, 8, 128),
            vm(2, 70, 80, 128),
            vm(2, 70, 80, 128),
            vm(2, 70, 80, 128),
            vm(*full),
            vm(3, 2, 4, 2, 24, 128),
            vm(3, 4, 4, 24, 128),
            vm(3, 2, 2, 4, 16, 128),
            vm(3, 4, 24, 128),
            vm(3, 4, 24, 128),
            vm(3, 2, 2, 16, 128),
            vm(3, 24, 128),
            vm(3, 24, 128),
            vm(3, 16, 128),
            vm(2, 4, 2, 24, 128),
            vm(4, 4, 24, 128),
            vm(2, 2, 4, 16, 128),
            vm(4, 24, 128),
            vm(4, 24, 128),
            vm(2, 2, 16, 128),
            vm(64, 128),
            vm(2, 8, 64, 128),
            pltpu.SemaphoreType.DMA((SEMS,)),
            pltpu.SemaphoreType.DMA((SEMS,)),
        ],
        compiler_params=pltpu.CompilerParams(
            collective_id=1, has_side_effects=True, vmem_limit_bytes=56 << 20
        ),
        name="response",
    )(orbitals, veff, trials, table, band)


def solution(mesh):
    placed = (
        P("orb", "dom", None, None),
        P("dom", None, None),
        P("orb", "dom", None, None),
        P(),
        P(),
        P("orb"),
    )
    return jax.shard_map(
        per_device,
        mesh=mesh,
        in_specs=placed,
        out_specs=P("orb", "dom", None, None),
        check_vma=False,
    )
```

time: 522 us -> 150 us (0.29)
  waiting for transfers between devices: 270 us -> 0 us
  Pallas kernels: 0 us -> 145 us
  other arithmetic: 144 us -> 1.55 us
  starting transfers between devices: 54.3 us -> 0 us
  blocking collectives: 20.7 us -> 0 us
  between operations: 17.7 us -> 0.02 us
  local copies, waits for them, and re-layouts: 14.1 us -> 2.86 us
    psum x2 -> x0, waiting for transfers between devices: 264 us -> none  [the longest x1 144 us: per_device(): responses.append(lax.psum(local_sum, 'orb'))]
    pallas_call x0 -> x1, Pallas kernels: none -> 145 us  [per_device(): pl.pallas_call(kernel, out_shape=jax.ShapeDtypeStruct((1, 8, 64, 128), f3...]
    ppermute x16 -> x0, starting transfers between devices: 54.2 us -> none  [the longest x8 43.7 us: extended_2(): lax.ppermute(lax.slice_in_dim(block, block.shape[dim] - width, None, axis...]
    reduce_sum x3 -> x0, other arithmetic: 41.1 us -> none  [the longest x2 39.4 us: per_device(): local_sum = jnp.sum(orbitals * deltas, axis=0)]
    concatenate x8 -> x1, other arithmetic: 37.1 us -> 0.01 us  [per_device(): jnp.concatenate([coefficients(level_gaps, orbital_count), masks[None]], a...]
    sub x4 -> x0, other arithmetic: 36.6 us -> none  [sweep_single(): following = 2.0 * image - previous]
    mul x8 -> x1, other arithmetic: 24.6 us -> 0.02 us  [coefficients(): d4 * (beta ** 4 * 4.0 / orbital_count)]
    psum x1 -> x0, blocking collectives: 20.7 us -> none  [per_device(): trial_total = lax.psum(jnp.sum(received * received), 'dom')]
  transfers between devices with their start and end apart: 18 -> 0, of which waited for: 6 -> 0; matrix products, arithmetic and copies ran while one was open for 20% -> 0% of each run, Pallas kernels for 0% -> 0%
where the time goes in v1:
time: 150 us
  Pallas kernels  145 us (97%)
  local copies, waits for them, and re-layouts  2.86 us (2%)
  other arithmetic  1.55 us (1%)
    pallas_call x1, Pallas kernels, per_device(): pl.pallas_call(kernel, out_shape=jax.ShapeDtypeStruct((1, 8, 64, 128), f3...  145 us

profile of v1, /device:TPU:1, one launch (start us, length us, event | category | flops | bytes accessed | tf_op | source)
XLA Modules:
  0.0 149.6 jit_solution(10056662325247524890)
XLA Ops:
  0.0 0.7 broadcast_compare_fusion
  0.7 0.9 select_reduce_fusion
  1.6 0.1 copy.17
  1.6 0.1 copy.13
  1.7 0.1 copy.16
  1.8 0.1 copy.15
  1.9 0.1 copy.14
  2.0 0.1 stack.2
  2.1 0.7 broadcast_in_dim.31.table
  2.8 145.2 %response.1 = f32[1,8,64,128]{3,2,1,0:T(8,128)} custom-call(f32[8,8,64,128]{3,2,1,0:T(8,128)} %orbitals.1, f32[8,64,128]{2,1,0:T(8,128)} %veff.1, f32[1,8,64,128]{3,2,1,0:T(8,128)} %trials.1, f32[9,8,128]{2,1,0:T(8,128)} %broadcast_in_dim.31.table, bf16[256,128]{1,0:T(8,128)(2,1)} %constant.46.clone.band), custom_call_target="tpu_custom_call" | custom-call | tf_op jit(solution)/shard_map/response/pallas_call | solution.py:341
  147.9 1.7 %copy.19 = f32[1,8,64,128]{3,2,1,0:T(8,128)} copy(f32[1,8,64,128]{3,2,1,0:T(8,128)} %response.1) | data formatting | bytes 524288
  (5 shorter events, 0.0 us)

commit v2 on v1

v2 whole, which is shorter than its diff:
```python
import functools

import jax
import jax.numpy as jnp
from jax import lax
from jax.experimental import pallas as pl
from jax.experimental.pallas import tpu as pltpu
from jax.sharding import PartitionSpec as P

APPS = 2
SWEEPS = 4
MESH = pl.DeviceIdType.MESH

taps = (135.0, -13.5, 1.0)
inverse_half = 1.0 / 5.05
center_depth = 5.05
norm_epsilon = 1e-06
beta = -0.5 * inverse_half / 90.0
center_rest = 49.0 / 12.0 - 4.05

XP, YP, ZP = 2, 1, 0
GROUPS = ((0, 24), (24, 24), (48, 16))


def place():
    orb, dom = lax.axis_index("orb"), lax.axis_index("dom")
    return dom % 4, dom // 4, orb // 8, (orb // 2) % 4, orb % 2


def device(x, y, z, c):
    return ((y % 2) * 8 + z * 2 + c, (y // 2) * 4 + x)


class Copies:
    def __init__(self, send, recv):
        self.send, self.recv, self.count = send, recv, 0

    def remote(self, src, dst, target):
        at = self.count
        self.count += 1
        copy = pltpu.make_async_remote_copy(
            src_ref=src,
            dst_ref=dst,
            send_sem=self.send.at[at],
            recv_sem=self.recv.at[at],
            device_id=target,
            device_id_type=MESH,
        )
        copy.start()
        return copy

    def local(self, src, dst):
        at = self.count
        self.count += 1
        copy = pltpu.make_async_copy(src, dst, self.send.at[at])
        copy.start()
        return copy


SEMS = 160


def kernel(
    orbitals, veff, trials, owners, levels, shift_index, out,
    phi, vfull, geff, masked, scattered, coef, band, fields, work_a, work_b, resp,
    r0a, r1a, r2a, r0b, r1b, r2b, r0c, r1c, r2c, s0a, s1a, s2a, s0b, s1b, s2b, final, slabs, z_a, z_b,
    send, recv,
):
    x, yh, yl, z, c = place()
    y = 2 * yh + yl
    orb, dom = lax.axis_index("orb"), lax.axis_index("dom")
    own = yl * 4 + z
    copies = Copies(send, recv)

    def along(dim, r):
        if dim == XP:
            return device((x + r) % 4, y, z, c)
        if dim == YP:
            return device(x, (y + r) % 4, z, c)
        return device(x, y, (z + r) % 4, c)

    sibling = device(x, y, z, 1 - c)

    barrier = pltpu.get_barrier_semaphore()
    peers = [((orb + r) % 16, dom) for r in range(1, 16)]
    peers += [(orb, (dom + r) % 8) for r in range(1, 8)]
    peers += [along(YP, 1), along(YP, 3)]
    for peer in peers:
        pl.semaphore_signal(barrier, inc=1, device_id=peer, device_id_type=MESH)
    pl.semaphore_wait(barrier, len(peers))

    chosen = [jnp.where(owners[app] == orb, 1.0, 0.0) for app in range(APPS)]
    for app in range(APPS):
        for i in range(8):
            masked[app, i] = trials[0, i] * chosen[app]
    spread = []
    for r in range(1, 16):
        to = (orb + r) % 16
        spread.append(copies.remote(masked.at[to % 2, to // 2], scattered.at[orb], (to, dom)))
    half = pl.ds(c * 32, 32)
    turn = 1 + 2 * yl
    order_y = (turn, 4 - turn, 2)

    def along_y(r):
        return device(x, (y + r) % 4, z, c)

    piece = veff.at[own, half]
    veff_y = [copies.remote(piece, geff.at[yh, x, yl, z, half], along_y(r)) for r in order_y]
    veff_own = copies.local(piece, geff.at[yh, x, yl, z, half])

    def move(flip, r):
        to = ((yh + flip) % 2) * 4 + (x + r) % 4
        source = ((yh + flip) % 2) * 4 + (x + 4 - r) % 4
        return source, copies.remote(orbitals.at[to], phi.at[c, dom], (orb, to))

    moved_near = [move(0, r) for r in (2, 1, 3)]
    phi_own = copies.local(orbitals.at[dom], phi.at[c, dom])
    phi_pair = [copies.remote(orbitals.at[dom], phi.at[c, dom], sibling)]
    gap = jnp.zeros((8, 128), jnp.float32) + levels[shift_index[dom]]
    for j, term in enumerate(coefficients(gap, 8 * 16)):
        coef[c, 8 * j : 8 * j + 8] = term
    coef_pair = copies.remote(coef.at[c], coef.at[c], sibling)
    distance = jnp.abs(
        lax.broadcasted_iota(jnp.int32, (256, 128), 0) % 128 - lax.broadcasted_iota(jnp.int32, (256, 128), 1)
    )
    band[...] = jnp.where(
        distance == 1, taps[0], jnp.where(distance == 2, taps[1], jnp.where(distance == 3, taps[2], 0.0))
    ).astype(jnp.bfloat16)

    zero_rows = jnp.zeros((8, 128), jnp.float32)
    zero_plane = jnp.zeros((80, 128), jnp.float32)
    for buffer in (fields, work_a, work_b):
        for k in range(2):
            for p in (0, 1, 2, 67, 68, 69):
                buffer[k, p] = zero_plane

            def border(p, carry, buffer=buffer, k=k):
                buffer[k, p, 0:8] = zero_rows
                buffer[k, p, 72:80] = zero_rows
                return carry

            lax.fori_loop(3, 67, border, 0)

    def wait(group):
        for copy in group:
            copy.wait()

    def ring(ref, h, rows):
        block = ref.at[h, :, :, z] if rows is None else ref.at[h, :, :, z, rows]
        return [copies.remote(block, block, along(ZP, r)) for r in (1, 3)]

    def relay(ref, h, rows, sends):
        wait(sends)
        started = []
        for l, zz, r in ((0, (z + 3) % 4, 1), (1, (z + 1) % 4, 3)):
            block = ref.at[h, :, l, zz] if rows is None else ref.at[h, :, l, zz, rows]
            started.append(copies.remote(block, block, along(ZP, r)))
        return started

    def forward(moves):
        for source, copy in moves:
            copy.wait()
            block = phi.at[c, source]
            phi_pair.append(copies.remote(block, block, sibling))

    other = 1 - yh

    def share(ref, h, rows):
        block = ref.at[h, x, :, z] if rows is None else ref.at[h, x, :, z, rows]
        return [copies.remote(block, block, along(XP, r)) for r in (2, 1, 3)]

    veff_own.wait()
    veff_y[0].wait()
    gx_own = share(geff, yh, half)
    wait(veff_y[1:])
    gx_oth = share(geff, other, half)
    scattered[orb] = masked[c, own]
    wait(spread)
    total = scattered[0]
    for g in range(1, 16):
        total = total + scattered[g]
    vfull[yh, x, yl, z] = total
    block = vfull.at[yh, x, yl, z]
    v_y = [copies.remote(block, block, along_y(r)) for r in order_y]
    wait(gx_own)
    g_own = ring(geff, yh, half)
    v_y[0].wait()
    vx_own = share(vfull, yh, None)
    wait(v_y[1:])
    vx_oth = share(vfull, other, None)
    moved_far = [move(1, 0)]
    wait(gx_oth)
    g_oth = ring(geff, other, half)
    wait(vx_own)
    v_own = ring(vfull, yh, None)
    wait(vx_oth)
    v_oth = ring(vfull, other, None)
    moved_far += [move(1, r) for r in (2, 1, 3)]
    g_own = relay(geff, yh, half, g_own)
    forward(moved_near)
    v_own = relay(vfull, yh, None, v_own)
    wait(g_own)
    block = geff.at[yh, :, :, :, half]
    g_pair = [copies.remote(block, block, sibling)]
    g_oth = relay(geff, other, half, g_oth)
    wait(v_own)
    phi_own.wait()
    wait(phi_pair)
    del phi_pair[:]
    coef_pair.wait()
    wait(g_pair)

    def start(p, norm):
        h, a, b, d = p // 32, (p // 8) % 4, (p // 4) % 2, p % 4
        v = vfull[h, a, b, d]
        for k in range(2):
            fields[k, p + 3, 8:72] = v * phi[k, p // 8, p % 8]
        geff[h, a, b, d] = (geff[h, a, b, d] + center_rest) * -180.0
        sq = v * v
        return norm + jnp.sum(sq.reshape(8, 8, 128), axis=0)

    def product(k, s, buf, src):
        block = src[k, pl.ds(s * 4 + 3, 4), 8:72].reshape(256, 128)
        high = block.astype(jnp.bfloat16)
        low = (block - high.astype(jnp.float32)).astype(jnp.bfloat16)
        buf[...] = jnp.dot(
            jnp.concatenate([high, low], axis=1), band[...], preferred_element_type=jnp.float32
        )

    def combine(k, s, buf, src, step, store):
        h, a, b = s // 8, (s // 2) % 4, s % 2
        weight = coef[k, step * 8 : step * 8 + 8]
        for r in range(0, 64, 8):
            column = [src[k, s * 4 + i, 8 + r : 16 + r] for i in range(10)]
            for i in range(4):
                value = column[i + 3]
                acc = buf[i * 64 + r : i * 64 + r + 8] + geff[h, a, b, i, r : r + 8] * value
                f = value if src is fields else fields[k, s * 4 + i + 3, 8 + r : 16 + r]
                acc = acc + weight * f
                for j in (1, 2, 3):
                    near = (column[i + 3 + j] + column[i + 3 - j]) + (
                        src[k, s * 4 + i + 3, 8 + r + j : 16 + r + j]
                        + src[k, s * 4 + i + 3, 8 + r - j : 16 + r - j]
                    )
                    acc = acc + (near if j == 3 else near * taps[j - 1])
                store(k, s, i, r, acc)

    def sweep(step, first, count):
        src, dst = ((fields, work_a), (work_a, work_b), (work_b, work_a), (work_a, None))[step]

        def keep(k, s, i, r, value):
            dst[k, s * 4 + i + 3, 8 + r : 16 + r] = value

        def respond(k, s, i, r, value):
            at = (s // 8, (s // 2) % 4, s % 2, i, slice(r, r + 8))
            value = value * (coef[k, 32:40] * phi[k, s // 2, (s % 2) * 4 + i, r : r + 8])
            resp[at] = value if k == 0 else resp[at] + value

        store = respond if dst is None else keep
        product(0, first, z_a, src)

        def chunk(n, carry):
            s = first + n
            product(1, s, z_b, src)
            combine(0, s, z_a, src, step, store)
            product(0, first + jnp.minimum(n + 1, count - 1), z_a, src)
            combine(1, s, z_b, src, step, store)
            return carry

        lax.fori_loop(0, count, chunk, 0)

    norm = jnp.zeros((8, 128), jnp.float32)

    def advance(step, done, until):
        sweep(step, jnp.where(yh == 0, done, 16 - until), until - done)

    norm = lax.fori_loop(32 * yh, 32 * yh + 32, start, norm)
    advance(0, 0, 7)
    v_oth = relay(vfull, other, None, v_oth)
    advance(1, 0, 6)
    wait(g_oth)
    block = geff.at[other, :, :, :, half]
    g_pair = [copies.remote(block, block, sibling)]
    forward(moved_far[:2])
    advance(2, 0, 5)
    forward(moved_far[2:])
    advance(3, 0, 4)
    wait(v_oth)
    wait(g_pair)
    wait(phi_pair)
    norm = lax.fori_loop(32 * other, 32 * other + 32, start, norm)
    for step in range(4):
        advance(step, 7 - step, 11 - step)
    scale = lax.rsqrt(jnp.sum(norm, keepdims=True) * (1.0 / 524288) + norm_epsilon)
    def part(dim, r, ref, kept):
        if dim == XP:
            where = {"x": (x + r) % 4}
        elif dim == YP:
            to = (y + r) % 4
            where = {"yh": to // 2, "yl": to % 2}
        else:
            where = {"z": (z + r) % 4}
        return ref.at[tuple(where.get(name, slice(None)) for name in kept)]

    names = {XP: ("x",), YP: ("yh", "yl"), ZP: ("z",)}
    orders = ((ZP, YP, XP), (YP, XP, ZP), (XP, ZP, YP))
    stages = ((r0a, r1a, r2a), (r0b, r1b, r2b), (r0c, r1c, r2c))
    sums = ((s0a, s1a, s2a), (s0b, s1b, s2b))
    kept = [("yh", "x", "yl", "z") for _ in GROUPS]
    current = [resp.at[:, :, :, :, first : first + count] for first, count in GROUPS]
    started = [[], [], []]

    def leave(h, turns):
        rows = [pl.ds(first, count) for first, count in GROUPS]
        for r in (2, 1, 3):
            started[0].append(
                copies.remote(resp.at[h, :, :, (z + r) % 4, rows[0]], r0a.at[r - 1, h], along(ZP, r))
            )
            started[2].append(
                copies.remote(resp.at[h, (x + r) % 4, :, :, rows[2]], r2a.at[r - 1, h], along(XP, r))
            )
        for r in turns:
            started[1].append(copies.remote(part(YP, r, current[1], kept[1]), r1a.at[r - 1], along_y(r)))

    leave(yh, (turn,))
    for step in range(4):
        advance(step, 11 - step, 16)
    leave(other, (4 - turn, 2))
    scale = lax.rsqrt(jnp.sum(norm, keepdims=True) * (1.0 / 524288) + norm_epsilon)
    for stage in range(3):
        if stage > 0:
            started = []
            for q in range(3):
                dim = orders[q][stage]
                started.append(
                    [
                        copies.remote(part(dim, r, current[q], kept[q]), stages[stage][q].at[r - 1], along(dim, r))
                        for r in (2, 1, 3)
                    ]
                )
        for q in range(3):
            dim = orders[q][stage]
            wait(started[q])
            received = stages[stage][q]
            mine = part(dim, 0, current[q], kept[q])
            kept[q] = tuple(name for name in kept[q] if name not in names[dim])
            first, count = GROUPS[q]
            if stage == 2:
                final[first : first + count] = ((mine[...] + received[0]) + (received[1] + received[2])) * scale
            else:
                sums[stage][q][...] = (mine[...] + received[0]) + (received[1] + received[2])
                current[q] = sums[stage][q]

    slabs[c, own] = final[...]
    shared, passed = [], [copies.remote(final, slabs.at[c, own], sibling)]
    for r in range(1, 8):
        to = (own + r) % 8
        shared.append(copies.remote(final, slabs.at[c, own], (to * 2 + c, dom)))
    for r in range(1, 8):
        shared[r - 1].wait()
        block = slabs.at[c, (own - r + 8) % 8]
        passed.append(copies.remote(block, block, sibling))
    wait(passed)
    for i in range(8):
        out[0, i] = slabs[0, i] * chosen[0] + slabs[1, i] * chosen[1]


def coefficients(level_gap, orbital_count):
    ratio_q = (center_depth + level_gap) * inverse_half
    root_term = jnp.sqrt(ratio_q * ratio_q - 1.0)
    decay = ratio_q - root_term
    c0 = -inverse_half / root_term
    c1 = c0 * (-2.0 * decay)
    c2 = c1 * -decay
    c3 = c2 * -decay
    c4 = c3 * -decay
    d0, d1, d2, d3, d4 = c0 - c2 + c4, c1 - 3.0 * c3, 2.0 * c2 - 8.0 * c4, 4.0 * c3, 8.0 * c4
    inverse = 1.0 / d4
    return [
        d3 * inverse * (1.0 / beta),
        d2 * inverse * (1.0 / beta**2),
        d1 * inverse * (1.0 / beta**3),
        d0 * inverse * (1.0 / beta**4),
        d4 * (beta**4 * 4.0 / orbital_count),
    ]


def per_device(orbitals, veff, trials, owners, levels, shift_index):
    f32 = jnp.float32
    vm = lambda *shape: pltpu.VMEM(shape, f32)
    full = (2, 4, 2, 4, 64, 128)
    return pl.pallas_call(
        kernel,
        out_shape=jax.ShapeDtypeStruct((1, 8, 64, 128), f32),
        in_specs=[
            pl.BlockSpec(memory_space=pl.ANY),
            pl.BlockSpec(memory_space=pl.ANY),
            pl.BlockSpec(memory_space=pltpu.VMEM),
            pl.BlockSpec(memory_space=pltpu.SMEM),
            pl.BlockSpec(memory_space=pltpu.SMEM),
            pl.BlockSpec(memory_space=pltpu.SMEM),
        ],
        out_specs=pl.BlockSpec(memory_space=pltpu.VMEM),
        scratch_shapes=[
            vm(2, 8, 8, 64, 128),
            vm(*full),
            vm(*full),
            vm(2, 8, 64, 128),
            vm(16, 64, 128),
            vm(2, 40, 128),
            pltpu.VMEM((256, 128), jnp.bfloat16),
            vm(2, 70, 80, 128),
            vm(2, 70, 80, 128),
            vm(2, 70, 80, 128),
            vm(*full),
            vm(3, 2, 4, 2, 24, 128),
            vm(3, 4, 4, 24, 128),
            vm(3, 2, 2, 4, 16, 128),
            vm(3, 4, 24, 128),
            vm(3, 4, 24, 128),
            vm(3, 2, 2, 16, 128),
            vm(3, 24, 128),
            vm(3, 24, 128),
            vm(3, 16, 128),
            vm(2, 4, 2, 24, 128),
            vm(4, 4, 24, 128),
            vm(2, 2, 4, 16, 128),
            vm(4, 24, 128),
            vm(4, 24, 128),
            vm(2, 2, 16, 128),
            vm(64, 128),
            vm(2, 8, 64, 128),
            vm(256, 128),
            vm(256, 128),
            pltpu.SemaphoreType.DMA((SEMS,)),
            pltpu.SemaphoreType.DMA((SEMS,)),
        ],
        compiler_params=pltpu.CompilerParams(
            collective_id=1, has_side_effects=True, vmem_limit_bytes=56 << 20
        ),
        name="response",
    )(orbitals, veff, trials, owners, levels, shift_index)


def solution(mesh):
    placed = (
        P("orb", "dom", None, None),
        P("dom", None, None),
        P("orb", "dom", None, None),
        P(),
        P(),
        P("orb"),
    )
    return jax.shard_map(
        per_device,
        mesh=mesh,
        in_specs=placed,
        out_specs=P("orb", "dom", None, None),
        check_vma=False,
    )
```

time: 150 us -> 109 us (0.73)
  Pallas kernels: 145 us -> 107 us
  other arithmetic: 1.55 us -> 0 us
    pallas_call x1, Pallas kernels: 145 us -> 107 us  [per_device(): pl.pallas_call(kernel, out_shape=jax.ShapeDtypeStruct((1, 8, 64, 128), f3...]
where the time goes in v2:
time: 109 us; the launch traced here: 108 us
  Pallas kernels  107 us (98%)
  local copies, waits for them, and re-layouts  1.67 us (2%)
    pallas_call x1, Pallas kernels, per_device(): pl.pallas_call(kernel, out_shape=jax.ShapeDtypeStruct((1, 8, 64, 128), f3...  107 us

profile of v2, /device:TPU:1, one launch (start us, length us, event | category | flops | bytes accessed | tf_op | source)
XLA Modules:
  0.0 108.4 jit_solution(93339352514731873)
XLA Ops:
  0.0 106.7 %response.1 = f32[1,8,64,128]{3,2,1,0:T(8,128)} custom-call(f32[8,8,64,128]{3,2,1,0:T(8,128)} %orbitals.1, f32[8,64,128]{2,1,0:T(8,128)} %veff.1, f32[1,8,64,128]{3,2,1,0:T(8,128)} %trials.1, s32[2]{0:T(128)} %owners.1, f32[8]{0:T(128)} %levels.1, s32[8]{0:T(128)} %shift_index.1), custom_call_target="tpu_custom_call" | custom-call | tf_op jit(solution)/shard_map/response/pallas_call | solution.py:392
  106.7 1.7 %copy.8 = f32[1,8,64,128]{3,2,1,0:T(8,128)} copy(f32[1,8,64,128]{3,2,1,0:T(8,128)} %response.1) | data formatting | bytes 524288

commit v3 on v2

--- a/solution.py
+++ b/solution.py
@@ -87,12 +87,11 @@
     peers += [along(YP, 1), along(YP, 3)]
     for peer in peers:
         pl.semaphore_signal(barrier, inc=1, device_id=peer, device_id_type=MESH)
-    pl.semaphore_wait(barrier, len(peers))
-
     chosen = [jnp.where(owners[app] == orb, 1.0, 0.0) for app in range(APPS)]
     for app in range(APPS):
         for i in range(8):
             masked[app, i] = trials[0, i] * chosen[app]
+    pl.semaphore_wait(barrier, len(peers))
     spread = []
     for r in range(1, 16):
         to = (orb + r) % 16
@@ -194,11 +193,11 @@
     wait(vx_own)
     v_own = ring(vfull, yh, None)
     wait(vx_oth)
-    v_oth = ring(vfull, other, None)
     moved_far += [move(1, r) for r in (2, 1, 3)]
     g_own = relay(geff, yh, half, g_own)
+    v_own = relay(vfull, yh, None, v_own)
+    v_oth = ring(vfull, other, None)
     forward(moved_near)
-    v_own = relay(vfull, yh, None, v_own)
     wait(g_own)
     block = geff.at[yh, :, :, :, half]
     g_pair = [copies.remote(block, block, sibling)]
@@ -310,22 +309,35 @@
     current = [resp.at[:, :, :, :, first : first + count] for first, count in GROUPS]
     started = [[], [], []]
 
-    def leave(h, turns):
+    def leave(h, xs, count, turns):
+        xs = pl.ds(xs, count)
         rows = [pl.ds(first, count) for first, count in GROUPS]
         for r in (2, 1, 3):
             started[0].append(
-                copies.remote(resp.at[h, :, :, (z + r) % 4, rows[0]], r0a.at[r - 1, h], along(ZP, r))
-            )
-            started[2].append(
-                copies.remote(resp.at[h, (x + r) % 4, :, :, rows[2]], r2a.at[r - 1, h], along(XP, r))
+                copies.remote(resp.at[h, xs, :, (z + r) % 4, rows[0]], r0a.at[r - 1, h, xs], along(ZP, r))
             )
         for r in turns:
-            started[1].append(copies.remote(part(YP, r, current[1], kept[1]), r1a.at[r - 1], along_y(r)))
-
-    leave(yh, (turn,))
+            to = (y + r) % 4
+            started[1].append(
+                copies.remote(resp.at[to // 2, xs, to % 2, :, rows[1]], r1a.at[r - 1, xs], along_y(r))
+            )
+
+    def leave_x(h):
+        for r in (2, 1, 3):
+            rows = pl.ds(GROUPS[2][0], GROUPS[2][1])
+            started[2].append(
+                copies.remote(resp.at[h, (x + r) % 4, :, :, rows], r2a.at[r - 1, h], along(XP, r))
+            )
+
+    leave(yh, 0, 4, (turn,))
+    leave_x(yh)
     for step in range(4):
-        advance(step, 11 - step, 16)
-    leave(other, (4 - turn, 2))
+        advance(step, 11 - step, 15 - step)
+    leave(other, 2 * yh, 2, (2, 4 - turn))
+    for step in range(4):
+        advance(step, 15 - step, 16)
+    leave(other, 2 - 2 * yh, 2, (2, 4 - turn))
+    leave_x(other)
     scale = lax.rsqrt(jnp.sum(norm, keepdims=True) * (1.0 / 524288) + norm_epsilon)
     for stage in range(3):
         if stage > 0:

time: 109 us -> 102 us (0.936)
  Pallas kernels: 107 us -> 100 us
    pallas_call x1, Pallas kernels: 107 us -> 100 us  [per_device(): pl.pallas_call(kernel, out_shape=jax.ShapeDtypeStruct((1, 8, 64, 128), f3...]
where the time goes in v3:
time: 102 us
  Pallas kernels  100 us (98%)
  local copies, waits for them, and re-layouts  1.67 us (2%)
    pallas_call x1, Pallas kernels, per_device(): pl.pallas_call(kernel, out_shape=jax.ShapeDtypeStruct((1, 8, 64, 128), f3...  100 us

profile of v3, /device:TPU:1, one launch (start us, length us, event | category | flops | bytes accessed | tf_op | source)
XLA Modules:
  0.0 101.7 jit_solution(13981710972920526931)
XLA Ops:
  0.0 100.0 %response.1 = f32[1,8,64,128]{3,2,1,0:T(8,128)} custom-call(f32[8,8,64,128]{3,2,1,0:T(8,128)} %orbitals.1, f32[8,64,128]{2,1,0:T(8,128)} %veff.1, f32[1,8,64,128]{3,2,1,0:T(8,128)} %trials.1, s32[2]{0:T(128)} %owners.1, f32[8]{0:T(128)} %levels.1, s32[8]{0:T(128)} %shift_index.1), custom_call_target="tpu_custom_call" | custom-call | tf_op jit(solution)/shard_map/response/pallas_call | solution.py:404
  100.0 1.7 %copy.8 = f32[1,8,64,128]{3,2,1,0:T(8,128)} copy(f32[1,8,64,128]{3,2,1,0:T(8,128)} %response.1) | data formatting | bytes 524288

commit v4 on v3

--- a/solution.py
+++ b/solution.py
@@ -63,9 +63,11 @@
 def kernel(
     orbitals, veff, trials, owners, levels, shift_index, out,
     phi, vfull, geff, masked, scattered, coef, band, fields, work_a, work_b, resp,
-    r0a, r1a, r2a, r0b, r1b, r2b, r0c, r1c, r2c, s0a, s1a, s2a, s0b, s1b, s2b, final, slabs, z_a, z_b,
-    send, recv,
+    r0a, r1a, r2a, r0b, r1b, r2b, r0c, r1c, r2c, s0a, s1a, s2a, s0b, s1b, s2b, final, slabs, *rest,
 ):
+    send, recv = rest[-2:]
+    shifted = (rest[0:2], rest[2:4], rest[4:6], rest[6:8])
+    z_a, z_b = shifted[0]
     x, yh, yl, z, c = place()
     y = 2 * yh + yl
     orb, dom = lax.axis_index("orb"), lax.axis_index("dom")
@@ -244,8 +246,10 @@
                     acc = acc + (near if j == 3 else near * taps[j - 1])
                 store(k, s, i, r, acc)
 
-    def sweep(step, first, count):
-        src, dst = ((fields, work_a), (work_a, work_b), (work_b, work_a), (work_a, None))[step]
+    flow = ((fields, work_a), (work_a, work_b), (work_b, work_a), (work_a, None))
+
+    def storing(step):
+        dst = flow[step][1]
 
         def keep(k, s, i, r, value):
             dst[k, s * 4 + i + 3, 8 + r : 16 + r] = value
@@ -255,7 +259,27 @@
             value = value * (coef[k, 32:40] * phi[k, s // 2, (s % 2) * 4 + i, r : r + 8])
             resp[at] = value if k == 0 else resp[at] + value
 
-        store = respond if dst is None else keep
+        return respond if dst is None else keep
+
+    def chunk_of(n):
+        return jnp.where(yh == 0, n, 15 - n)
+
+    def wave(m, carry):
+        def dot(step, k, n):
+            product(k, chunk_of(n), shifted[step][k], flow[step][0])
+
+        def add(step, k):
+            combine(k, chunk_of(m + 3 - step), shifted[step][k], flow[step][0], step, storing(step))
+
+        for step, ahead, n in ((0, 2, m + 1), (1, 3, m), (2, 0, jnp.minimum(m + 4, 15)), (3, 1, jnp.minimum(m + 3, 15))):
+            for k in range(2):
+                dot(ahead, k, n)
+                add(step, k)
+        return carry
+
+    def sweep(step, first, count):
+        src, dst = flow[step]
+        store = storing(step)
         product(0, first, z_a, src)
 
         def chunk(n, carry):
@@ -288,8 +312,10 @@
     wait(g_pair)
     wait(phi_pair)
     norm = lax.fori_loop(32 * other, 32 * other + 32, start, norm)
-    for step in range(4):
-        advance(step, 7 - step, 11 - step)
+    for step in range(2):
+        for k in range(2):
+            product(k, chunk_of(7 - step), shifted[step][k], flow[step][0])
+    lax.fori_loop(4, 8, wave, 0)
     scale = lax.rsqrt(jnp.sum(norm, keepdims=True) * (1.0 / 524288) + norm_epsilon)
     def part(dim, r, ref, kept):
         if dim == XP:
@@ -331,11 +357,11 @@
 
     leave(yh, 0, 4, (turn,))
     leave_x(yh)
-    for step in range(4):
-        advance(step, 11 - step, 15 - step)
+    lax.fori_loop(8, 12, wave, 0)
     leave(other, 2 * yh, 2, (2, 4 - turn))
-    for step in range(4):
-        advance(step, 15 - step, 16)
+    lax.fori_loop(12, 13, wave, 0)
+    for step in (1, 2, 3):
+        advance(step, 16 - step, 16)
     leave(other, 2 - 2 * yh, 2, (2, 4 - turn))
     leave_x(other)
     scale = lax.rsqrt(jnp.sum(norm, keepdims=True) * (1.0 / 524288) + norm_epsilon)
@@ -442,8 +468,7 @@
             vm(2, 2, 16, 128),
             vm(64, 128),
             vm(2, 8, 64, 128),
-            vm(256, 128),
-            vm(256, 128),
+            *[vm(256, 128) for _ in range(8)],
             pltpu.SemaphoreType.DMA((SEMS,)),
             pltpu.SemaphoreType.DMA((SEMS,)),
         ],

time: 102 us -> 99.5 us (0.975)
  Pallas kernels: 100 us -> 97.7 us
    pallas_call x1, Pallas kernels: 100 us -> 97.7 us  [per_device(): pl.pallas_call(kernel, out_shape=jax.ShapeDtypeStruct((1, 8, 64, 128), f3...]
where the time goes in v4:
time: 99.5 us; the launch traced here: 99.4 us
  Pallas kernels  97.7 us (98%)
  local copies, waits for them, and re-layouts  1.67 us (2%)
    pallas_call x1, Pallas kernels, per_device(): pl.pallas_call(kernel, out_shape=jax.ShapeDtypeStruct((1, 8, 64, 128), f3...  97.7 us

profile of v4, /device:TPU:1, one launch (start us, length us, event | category | flops | bytes accessed | tf_op | source)
XLA Modules:
  0.0 99.4 jit_solution(6538234141993925565)
XLA Ops:
  0.0 97.7 %response.1 = f32[1,8,64,128]{3,2,1,0:T(8,128)} custom-call(f32[8,8,64,128]{3,2,1,0:T(8,128)} %orbitals.1, f32[8,64,128]{2,1,0:T(8,128)} %veff.1, f32[1,8,64,128]{3,2,1,0:T(8,128)} %trials.1, s32[2]{0:T(128)} %owners.1, f32[8]{0:T(128)} %levels.1, s32[8]{0:T(128)} %shift_index.1), custom_call_target="tpu_custom_call" | custom-call | tf_op jit(solution)/shard_map/response/pallas_call | solution.py:430
  97.7 1.7 %copy.8 = f32[1,8,64,128]{3,2,1,0:T(8,128)} copy(f32[1,8,64,128]{3,2,1,0:T(8,128)} %response.1) | data formatting | bytes 524288

commit v5 on v4

--- a/solution.py
+++ b/solution.py
@@ -300,13 +300,13 @@
     norm = lax.fori_loop(32 * yh, 32 * yh + 32, start, norm)
     advance(0, 0, 7)
     v_oth = relay(vfull, other, None, v_oth)
+    forward(moved_far[:1])
     advance(1, 0, 6)
     wait(g_oth)
     block = geff.at[other, :, :, :, half]
     g_pair = [copies.remote(block, block, sibling)]
-    forward(moved_far[:2])
+    forward(moved_far[1:])
     advance(2, 0, 5)
-    forward(moved_far[2:])
     advance(3, 0, 4)
     wait(v_oth)
     wait(g_pair)

time: 99.5 us -> 98.7 us (level)
  no operation moved by 1% of the time
where the time goes in v5:
time: 98.7 us; the launch traced here: 98.6 us
  Pallas kernels  96.9 us (98%)
  local copies, waits for them, and re-layouts  1.67 us (2%)
    pallas_call x1, Pallas kernels, per_device(): pl.pallas_call(kernel, out_shape=jax.ShapeDtypeStruct((1, 8, 64, 128), f3...  96.9 us

profile of v5, /device:TPU:1, one launch (start us, length us, event | category | flops | bytes accessed | tf_op | source)
XLA Modules:
  0.0 98.6 jit_solution(9200090930054165760)
XLA Ops:
  0.0 96.9 %response.1 = f32[1,8,64,128]{3,2,1,0:T(8,128)} custom-call(f32[8,8,64,128]{3,2,1,0:T(8,128)} %orbitals.1, f32[8,64,128]{2,1,0:T(8,128)} %veff.1, f32[1,8,64,128]{3,2,1,0:T(8,128)} %trials.1, s32[2]{0:T(128)} %owners.1, f32[8]{0:T(128)} %levels.1, s32[8]{0:T(128)} %shift_index.1), custom_call_target="tpu_custom_call" | custom-call | tf_op jit(solution)/shard_map/response/pallas_call | solution.py:430
  96.9 1.7 %copy.8 = f32[1,8,64,128]{3,2,1,0:T(8,128)} copy(f32[1,8,64,128]{3,2,1,0:T(8,128)} %response.1) | data formatting | bytes 524288
